TPU v7x, 256 devices: a whole 4x4x8 slice. The times are simulated.
256 devices in a mesh: span: 32 (over y, x, core), chord: 8 (over z).
Axes of the slice: x: 4, y: 4, z: 8, core: 2. Of those that a mesh axis runs over, the one named last changes fastest.
Arguments:
- right_side: float32 [162, 32768], P(None, ('span', 'chord')), may hold values from -8 to 8
- diag_blocks: bfloat16 [162, 162, 32768], P(None, None, ('span', 'chord')), may hold values from -0.25 to 3.1
- face_blocks: bfloat16 [6, 54, 54, 32768], P(None, None, None, ('span', 'chord')), may hold values from -0.29882812 to 0.29882812
- orient_codes: int32 [6, 32768], P(None, ('span', 'chord')), may hold values from 0 to 7
- live_counts: int32 [256], P(('span', 'chord')), may hold values from 1 to 128, 24576 in all
- shifts: float32 [4], replicated, may hold values from 0.8 to 2.5
- shift_order: int32 [4], replicated, may hold values from 0 to 3, each once
Outputs:
- adjoint: float32 [162, 32768], P(None, ('span', 'chord'))
- residual: float32 [162, 32768], P(None, ('span', 'chord'))
- coefficients: float32 [3, 4], replicated
Inputs may be any that keep to these rules, and one draw needn't show every extreme that they name: `live_counts`: each partition holds at least one live element, and some partition holds 128. `shift_order`: each value once.
All inputs are finite; a program needn't handle non-finite values. No bound on the sum of `live_counts` on one device may be relied on, other than what follows from the above.
Results may differ from a plain program's by a relative error of at most 0.0012.
Values sent between devices are 32-bit elements; how exact they have to be, the bound alone decides.
A program may use at most 128 MiB of HBM per device.

v0:
```python
import functools

import jax
import jax.numpy as jnp
from jax import lax
from jax.experimental import pallas as pl
from jax.experimental.pallas import tpu as pltpu
from jax.sharding import PartitionSpec as P

MESH = pl.DeviceIdType.MESH
F32 = jnp.float32

CYCLES = 3
STEPS = 4
AHEAD = 2
TOTAL = 12
BLOCK = 162
FACE = 54
NVAR = 6
ROWS = 168
ELEMS = 128
SPANS = 32
CHORDS = 8
GROUP = 16
ENTRIES = 15
CHUNK = 18
SPOTS = ((1, 0), (1, 2), (2, 0), (2, 2), (3, 0), (3, 2))


def node_of(face, s, t):
    axis_pos, spot = SPOTS[face]
    place = [s, t]
    place.insert(axis_pos - 1, spot)
    return place[0] * 9 + place[1] * 3 + place[2]


def pair_index(i, j):
    i, j = min(i, j), max(i, j)
    return i * 5 - i * (i - 1) // 2 + (j - i)


def kernel(
    rhs_hbm, diag_hbm, face_hbm, codes, live, shifts, order,
    adj_out, res_out, coef_out,
    dstage, fstage, diag, face, basis, adj, prod, result, local, sbuf, rbuf, gacc, slots,
    rhs_sem, dsem, fsem, send_sem, recv_sem, gsend_sem, grecv_sem,
):
    span, chord = lax.axis_index("span"), lax.axis_index("chord")
    core, chip = lax.rem(span, 2), span // 2

    rhs_copy = pltpu.make_async_copy(rhs_hbm, basis.at[0, pl.ds(0, BLOCK)], rhs_sem)
    rhs_copy.start()
    face_copies = {
        g: pltpu.make_async_copy(face_hbm.at[g], fstage.at[g], fsem.at[g]) for g in range(6)
    }
    for g in (2, 3, 0, 1, 4, 5):
        face_copies[g].start()

    def diag_copy(i):
        rows = pl.ds(i * CHUNK, CHUNK)
        return pltpu.make_async_copy(diag_hbm.at[rows], dstage.at[rows], dsem.at[i])

    for i in range(BLOCK // CHUNK):
        diag_copy(i).start()

    neighbours = (
        (lax.rem(span + SPANS - 1, SPANS), chord),
        (lax.rem(span + 1, SPANS), chord),
        (span, lax.rem(chord + CHORDS - 1, CHORDS)),
        (span, lax.rem(chord + 1, CHORDS)),
    )
    me_in = (chord * 2 + core, chip)

    def partner(phase, off):
        there = lax.rem(me_in[phase] + off, GROUP)
        if phase == 0:
            return (chip * 2 + lax.rem(there, 2), there // 2)
        return (there * 2 + core, chord)

    barrier = pltpu.get_barrier_semaphore()
    for to in neighbours[:2]:
        pl.semaphore_signal(barrier, inc=1, device_id=to, device_id_type=MESH)
    for phase in range(2):
        for off in range(1, GROUP):
            pl.semaphore_signal(
                barrier, inc=1, device_id=partner(phase, off), device_id_type=MESH
            )

    alive = lax.broadcasted_iota(jnp.int32, (8, ELEMS), 1) < live[0]
    alive6 = alive[:NVAR]
    lane6 = lax.broadcasted_iota(jnp.int32, (NVAR, ELEMS), 1)
    eye = lax.broadcasted_iota(jnp.int32, (GROUP, ELEMS), 0) == lax.broadcasted_iota(
        jnp.int32, (GROUP, ELEMS), 1
    )
    thetas = [shifts[order[k]] for k in range(STEPS)]
    keep = (
        (span > 0).astype(F32),
        (span < SPANS - 1).astype(F32),
        (chord > 0).astype(F32),
        (chord < CHORDS - 1).astype(F32),
    )

    for k in range(1, STEPS + AHEAD + 1):
        basis[k, pl.ds(160, 8), :] = jnp.zeros((8, ELEMS), F32)
    adj[...] = jnp.zeros_like(adj)
    gacc[...] = jnp.zeros_like(gacc)
    rhs_copy.wait()
    for i in range(0, 160, 8):
        basis[0, pl.ds(i, 8), :] = jnp.where(alive, basis[0, pl.ds(i, 8), :], 0.0)
    tail = jnp.where(alive[:2], basis[0, pl.ds(160, 2), :], 0.0)
    basis[0, pl.ds(160, 8), :] = jnp.zeros((8, ELEMS), F32)
    basis[0, pl.ds(160, 2), :] = tail

    def remote(step, g):
        return pltpu.make_async_remote_copy(
            src_ref=sbuf.at[step, g],
            dst_ref=rbuf.at[step, g ^ 1],
            send_sem=send_sem.at[step, g],
            recv_sem=recv_sem.at[step, g ^ 1],
            device_id=neighbours[g],
            device_id_type=MESH,
        )

    def face_products(k, faces, first):
        def some(v, sums):
            sums = list(sums)
            for j in range(9):
                for n, g in enumerate(faces):
                    if first:
                        block = fstage[g, v * 9 + j].astype(F32)
                        face[g, v * 9 + j] = block
                    else:
                        block = face[g, v * 9 + j]
                    row = v * 27 + node_of(g, j // 3, j % 3)
                    sums[n] = sums[n] + block * basis[k, pl.ds(row, 1), :]
            return tuple(sums)

        def body(i, sums):
            for u in range(3):
                sums = some(i * 3 + u, sums)
            return sums

        zero = tuple(jnp.zeros((FACE, ELEMS), F32) for _ in faces)
        return lax.fori_loop(0, NVAR // 3, body, zero)

    def oriented(g, product):
        prod[g, pl.ds(0, FACE), :] = product
        y = [[prod[g, pl.ds(3 * s + t, NVAR, stride=9), :] for t in range(3)] for s in range(3)]
        code = jnp.broadcast_to(codes[pl.ds(g, 1), :], (NVAR, ELEMS))
        swap, flip_s, flip_t = [(code & bit) != 0 for bit in (4, 1, 2)]
        y = [[y[s][t] if s == t else jnp.where(swap, y[t][s], y[s][t]) for t in range(3)] for s in range(3)]
        y = [[y[s][t] if s == 1 else jnp.where(flip_s, y[2 - s][t], y[s][t]) for t in range(3)] for s in range(3)]
        return [[y[s][t] if t == 1 else jnp.where(flip_t, y[s][2 - t], y[s][t]) for t in range(3)] for s in range(3)]

    def do_faces(step, k, faces, first):
        products = face_products(k, faces, first)
        for g, product in zip(faces, products):
            y = oriented(g, product)
            for s in range(3):
                for t in range(3):
                    if g < 4:
                        sbuf[step, g, pl.ds(3 * s + t, NVAR, stride=9), :] = y[s][t]
                    elif g == 5:
                        moved = pltpu.roll(y[s][t], 1, 1)
                        local[0, 3 * s + t] = jnp.where(lane6 == 0, 0.0, moved)
                    else:
                        moved = pltpu.roll(y[s][t], ELEMS - 1, 1)
                        local[1, 3 * s + t] = jnp.where(lane6 == ELEMS - 1, 0.0, moved)
            if g < 4:
                remote(step, g).start()

    def diag_product(k, first):
        def body(i, total):
            if first:
                diag_copy(i).wait()
            for u in range(CHUNK):
                p = i * CHUNK + u
                if first:
                    block = dstage[p].astype(F32)
                    diag[p] = block
                else:
                    block = diag[p]
                total = total + block * basis[k, pl.ds(p, 1), :]
            return total

        result[...] = lax.fori_loop(0, BLOCK // CHUNK, body, jnp.zeros((BLOCK, ELEMS), F32))

    def finish_product(step, k, theta):
        for g in range(4):
            remote(step, g).wait_recv()
        for a in range(3):
            for b in range(3):
                for c in range(3):
                    rows = pl.ds(9 * a + 3 * b + c, NVAR, stride=27)
                    value = result[rows, :]
                    for at, g, (s, t) in ((a, 0, (b, c)), (b, 2, (a, c))):
                        if at != 1:
                            side = g + at // 2
                            got = rbuf[step, side, pl.ds(3 * s + t, NVAR, stride=9), :]
                            value = value + got * keep[side]
                    if c != 1:
                        value = value + local[c // 2, 3 * a + b]
                    value = jnp.where(alive6, value, 0.0)
                    basis[k + 1, rows, :] = value - theta * basis[k, rows, :]
        for g in range(4):
            remote(step, g).wait_send()

    def product(step, k, theta, first):
        for pair in ((2, 3), (0, 1), (4, 5)):
            if first:
                for g in pair:
                    face_copies[g].wait()
                if pair == (2, 3):
                    pl.semaphore_wait(barrier, 2 * GROUP)
            do_faces(step, k, pair, first)
        diag_product(k, first)
        finish_product(step, k, theta)

    def phase_copy(cycle, phase, off, count=None):
        place = pl.ds(0, count) if count else me_in[phase]
        ref = slots.at[cycle, phase, place]
        return pltpu.make_async_remote_copy(
            src_ref=ref,
            dst_ref=ref,
            send_sem=gsend_sem.at[cycle, phase],
            recv_sem=grecv_sem.at[cycle, phase],
            device_id=partner(phase, off),
            device_id_type=MESH,
        )

    def send_phase(cycle, phase, row):
        slots[cycle, phase, me_in[phase]] = row
        for off in range(1, GROUP):
            phase_copy(cycle, phase, off).start()

    def take_phase(cycle, phase):
        copy = phase_copy(cycle, phase, 1, GROUP - 1)
        copy.wait_send()
        copy.wait_recv()
        return jnp.sum(slots[cycle, phase], axis=0)

    def start_gram(cycle):
        def body(i, sums):
            sums = list(sums)
            for u in range(3):
                v = [basis[k, pl.ds(pl.multiple_of(i * 24 + u * 8, 8), 8), :] for k in range(5)]
                for a in range(5):
                    for b in range(a, 5):
                        e = pair_index(a, b)
                        sums[e] = sums[e] + v[a] * v[b]
            return tuple(sums)

        sums = lax.fori_loop(
            0, ROWS // 24, body, tuple(jnp.zeros((8, ELEMS), F32) for _ in range(ENTRIES))
        )
        for e in range(ENTRIES):
            gacc[pl.ds(8 * e, 8), :] = sums[e]
        part = gacc[pl.ds(0, GROUP, stride=8), :]
        for r in range(1, 8):
            part = part + gacc[pl.ds(r, GROUP, stride=8), :]
        column = jnp.sum(part, axis=1, keepdims=True)
        row = jnp.sum(jnp.where(eye, column, 0.0), axis=0, keepdims=True)
        send_phase(cycle, 0, row)

    def middle_gram(cycle):
        send_phase(cycle, 1, take_phase(cycle, 0))

    def end_gram(cycle):
        row = take_phase(cycle, 1)
        spread = jnp.sum(jnp.where(eye, row, 0.0), axis=1, keepdims=True)
        spread = jnp.broadcast_to(spread, (GROUP, ELEMS))
        gram = [
            [spread[pair_index(i, j):pair_index(i, j) + 1] for j in range(5)] for i in range(5)
        ]
        half = [[gram[i][k] * thetas[k] + gram[i][k + 1] for k in range(4)] for i in range(5)]
        normal = [[half[j][k] * thetas[j] + half[j + 1][k] for k in range(4)] for j in range(4)]
        target = [gram[j][0] * thetas[j] + gram[j + 1][0] for j in range(4)]
        low = [[None] * 4 for _ in range(4)]
        scaled = [[None] * 4 for _ in range(4)]
        inverse = [None] * 4
        for j in range(4):
            for i in range(j, 4):
                value = normal[i][j]
                for m in range(j):
                    value = value - low[j][m] * scaled[i][m]
                scaled[i][j] = value
            inverse[j] = 1.0 / scaled[j][j]
            for i in range(j + 1, 4):
                low[i][j] = scaled[i][j] * inverse[j]
        fore = []
        for i in range(4):
            value = target[i]
            for m in range(i):
                value = value - low[i][m] * fore[m]
            fore.append(value)
        weights = [None] * 4
        for i in reversed(range(4)):
            value = fore[i] * inverse[i]
            for m in range(i + 1, 4):
                value = value - low[m][i] * weights[m]
            weights[i] = value
        combined = [weights[0] * thetas[0]]
        for i in range(1, 4):
            combined.append(weights[i] * thetas[i] + weights[i - 1])
        combined.append(weights[3])
        lanes = lax.broadcasted_iota(jnp.int32, (1, ELEMS), 1)
        line = jnp.zeros((1, ELEMS), F32)
        for i in range(4):
            line = jnp.where(lanes == i, weights[i], line)
        coef_out[pl.ds(cycle, 1), :] = line[:, :STEPS]
        return weights, combined

    def wide(values):
        return [jnp.broadcast_to(value, (8, ELEMS)) for value in values]

    def next_cycle(cycle):
        weights, combined = end_gram(cycle)
        weights8, combined8 = wide(weights), wide(combined)
        sets = [[1.0 - combined[0]] + [-value for value in combined[1:]]]
        for m in range(AHEAD):
            old = sets[-1]
            new = [None] * (len(old) + 1)
            for i, value in enumerate(old):
                here = value * (thetas[i % STEPS] - thetas[m])
                new[i] = here if new[i] is None else new[i] + here
                new[i + 1] = value
            sets.append(new)
        sets8 = [wide(one) for one in sets]

        def body(i, carry):
            rows = pl.ds(pl.multiple_of(i * 8, 8), 8)
            v = [basis[k, rows, :] for k in range(STEPS + AHEAD + 1)]
            total = adj[rows, :]
            for k in range(STEPS):
                total = total + weights8[k] * v[k]
            adj[rows, :] = total
            fresh = v[0]
            for k in range(STEPS + 1):
                fresh = fresh - combined8[k] * v[k]
            basis[0, rows, :] = fresh
            for m in range(1, AHEAD + 1):
                total = sets8[m][0] * v[0]
                for k in range(1, len(sets8[m])):
                    total = total + sets8[m][k] * v[k]
                basis[m, rows, :] = total
            return carry

        lax.fori_loop(0, ROWS // 8, body, 0)

    def last_cycle(cycle):
        weights, combined = end_gram(cycle)
        weights8, combined8 = wide(weights), wide(combined)
        for i in range(0, BLOCK, 8):
            size = min(8, BLOCK - i)
            rows = pl.ds(i, size)
            v = [basis[k, rows, :] for k in range(STEPS + 1)]
            total = adj[rows, :]
            for k in range(STEPS):
                total = total + weights8[k][:size] * v[k]
            adj_out[rows, :] = total
            fresh = v[0]
            for k in range(STEPS + 1):
                fresh = fresh - combined8[k][:size] * v[k]
            res_out[rows, :] = fresh

    product(0, 0, thetas[0], True)

    def step_body(step, carry):
        k = jnp.where(step < 2, step, lax.rem(step + 2, 4) + 2)
        product(step, k, shifts[order[lax.rem(k, STEPS)]], False)
        place = lax.rem(step, 4)
        cycle = step // 4

        @pl.when(place == 3)
        def _():
            start_gram(cycle)

        @pl.when(jnp.logical_and(place == 0, step >= 4))
        def _():
            middle_gram(cycle - 1)

        @pl.when(jnp.logical_and(place == 1, step >= 4))
        def _():
            next_cycle(cycle - 1)

        return carry

    lax.fori_loop(1, TOTAL, step_body, 0)
    middle_gram(CYCLES - 1)
    last_cycle(CYCLES - 1)


def on_device(right_side, diag_blocks, face_blocks, orient_codes, live_counts, shifts, shift_order):
    vmem = pl.BlockSpec(memory_space=pltpu.VMEM)
    smem = pl.BlockSpec(memory_space=pltpu.SMEM)
    anywhere = pl.BlockSpec(memory_space=pl.ANY)
    return pl.pallas_call(
        kernel,
        out_shape=(
            jax.ShapeDtypeStruct((BLOCK, ELEMS), F32),
            jax.ShapeDtypeStruct((BLOCK, ELEMS), F32),
            jax.ShapeDtypeStruct((CYCLES, STEPS), F32),
        ),
        in_specs=[anywhere, anywhere, anywhere, vmem, smem, smem, smem],
        out_specs=(vmem, vmem, vmem),
        scratch_shapes=[
            pltpu.VMEM((BLOCK, BLOCK, ELEMS), jnp.bfloat16),
            pltpu.VMEM((6, FACE, FACE, ELEMS), jnp.bfloat16),
            pltpu.VMEM((BLOCK, BLOCK, ELEMS), F32),
            pltpu.VMEM((6, FACE, FACE, ELEMS), F32),
            pltpu.VMEM((STEPS + AHEAD + 1, ROWS, ELEMS), F32),
            pltpu.VMEM((ROWS, ELEMS), F32),
            pltpu.VMEM((6, 56, ELEMS), F32),
            pltpu.VMEM((BLOCK, ELEMS), F32),
            pltpu.VMEM((2, 9, NVAR, ELEMS), F32),
            pltpu.VMEM((TOTAL, 4, FACE, ELEMS), F32),
            pltpu.VMEM((TOTAL, 4, FACE, ELEMS), F32),
            pltpu.VMEM((GROUP * 8, ELEMS), F32),
            pltpu.VMEM((CYCLES, 2, GROUP, 1, ELEMS), F32),
            pltpu.SemaphoreType.DMA,
            pltpu.SemaphoreType.DMA((BLOCK // CHUNK,)),
            pltpu.SemaphoreType.DMA((6,)),
            pltpu.SemaphoreType.DMA((TOTAL, 4)),
            pltpu.SemaphoreType.DMA((TOTAL, 4)),
            pltpu.SemaphoreType.DMA((CYCLES, 2)),
            pltpu.SemaphoreType.DMA((CYCLES, 2)),
        ],
        compiler_params=pltpu.CompilerParams(
            collective_id=0, has_side_effects=True, vmem_limit_bytes=56 * 2**20
        ),
    )(right_side, diag_blocks, face_blocks, orient_codes, live_counts, shifts, shift_order)


def solution(mesh):
    placed = (
        P(None, ("span", "chord")),
        P(None, None, ("span", "chord")),
        P(None, None, None, ("span", "chord")),
        P(None, ("span", "chord")),
        P(("span", "chord")),
        P(),
        P(),
    )
    return jax.shard_map(
        on_device,
        mesh=mesh,
        in_specs=placed,
        out_specs=(P(None, ("span", "chord")), P(None, ("span", "chord")), P()),
        check_vma=False,
    )
```

profile of v0, /device:TPU:1, one launch (start us, length us, event | category | flops | bytes accessed | tf_op | source)
XLA Modules:
  0.0 84.8 jit_solution(9643791302214562056)
XLA Ops:
  1.3 79.2 %shard_map.94 = (f32[162,128]{1,0:T(8,128)}, f32[162,128]{1,0:T(8,128)}, f32[3,4]{1,0:T(4,128)}) custom-call(f32[162,128]{1,0:T(8,128)} %rhs_hbm.1, bf16[162,162,128]{2,1,0:T(8,128)(2,1)} %diag_hbm.1, bf16[6,54,54,128]{3,2,1,0:T(8,128)(2,1)} %face_hbm.1, s32[6,128]{1,0:T(8,128)} %codes.1, s32[1]{0:T(128)S(6)} %copy.13.live, f32[4]{0:T(128)} %shifts.1, s32[4]{0:T(128)} %order.1), custom_call_target="tpu_custom_call" | custom-call | tf_op jit(solution)/shard_map/pallas_call | solution.py:397
  80.5 1.5 %copy.14 = f32[162,128]{1,0:T(8,128)} copy(f32[162,128]{1,0:T(8,128)} %get-tuple-element.6) | data formatting | bytes 165888
  82.0 1.5 %copy.15 = f32[162,128]{1,0:T(8,128)} copy(f32[162,128]{1,0:T(8,128)} %get-tuple-element.7) | data formatting | bytes 165888
  83.6 1.2 %copy.16 = f32[3,4]{1,0:T(4,128)} copy(f32[3,4]{1,0:T(4,128)} %get-tuple-element.8) | data formatting | bytes 96
where the time goes:
time: 85 us; the launch traced here: 84.8 us
  Pallas kernels  79.2 us (93%)
  local copies, waits for them, and re-layouts  4.29 us (5%)
  between operations  1.29 us (2%)
    pallas_call x1, Pallas kernels, on_device(): pl.pallas_call(kernel, out_shape=(jax.ShapeDtypeStruct((BLOCK, ELEMS), F3...  79.2 us
    unnamed x3, local copies, waits for them, and re-layouts  4.29 us

commit v1 on v0

v1 whole, which is shorter than its diff:
```python
import functools

import jax
import jax.numpy as jnp
from jax import lax
from jax.experimental import pallas as pl
from jax.experimental.pallas import tpu as pltpu
from jax.sharding import PartitionSpec as P

MESH = pl.DeviceIdType.MESH
F32 = jnp.float32

CYCLES = 3
STEPS = 4
AHEAD = 4
TOTAL = 12
BLOCK = 162
FACE = 54
NVAR = 6
NODES = 27
ELEMS = 128
SPANS = 32
CHORDS = 8
GROUP = 16
ENTRIES = 15
CHUNK = 27

def node_of(axis, side, j):
    if axis == 0:
        return side * 18 + j
    if axis == 1:
        return (j // 3) * 9 + side * 6 + j % 3
    return j * 3 + side * 2


def pair_index(i, j):
    i, j = min(i, j), max(i, j)
    return i * 5 - i * (i - 1) // 2 + (j - i)


def kernel(
    rhs_hbm, diag_hbm, face_hbm, codes_hbm, live_hbm, shifts_hbm, order_hbm,
    adj_out, res_out, coef_out,
    dstage, fstage, diag, face, rhs, codes, live, shifts, order, basis, adj, prod, result, local, masks, sbuf, rbuf,
    gacc, slots,
    small_sem, dsem, fsem, send_sem, recv_sem, gsend_sem, grecv_sem,
):
    span, chord = lax.axis_index("span"), lax.axis_index("chord")
    core, chip = lax.rem(span, 2), span // 2
    inner = (chord < CHORDS // 2).astype(jnp.int32)
    far, middle, outer, near = (0, core), (1, inner), (1, 1 - inner), (0, 1 - core)

    small_copies = [
        pltpu.make_async_copy(source, target, small_sem.at[i])
        for i, (source, target) in enumerate(
            (
                (rhs_hbm, rhs),
                (live_hbm, live),
                (codes_hbm, codes),
                (shifts_hbm, shifts),
                (order_hbm, order),
            )
        )
    ]
    for copy in small_copies[:2]:
        copy.start()

    def face_copy(axis, side):
        g = 2 * axis + side
        return pltpu.make_async_copy(face_hbm.at[g], fstage.at[g], fsem.at[g])

    face_copy(*far).start()
    for copy in small_copies[2:]:
        copy.start()
    for one in (middle, outer, near, (2, 0), (2, 1)):
        face_copy(*one).start()

    def diag_copy(i):
        rows = pl.ds(i * CHUNK, CHUNK)
        return pltpu.make_async_copy(diag_hbm.at[rows], dstage.at[rows], dsem.at[i])

    for i in range(BLOCK // CHUNK):
        diag_copy(i).start()

    def neighbour(axis, side):
        if axis == 0:
            return (lax.rem(span + SPANS + 2 * side - 1, SPANS), chord)
        return (span, lax.rem(chord + CHORDS + 2 * side - 1, CHORDS))

    def when_there(axis, side, act):
        place, count = ((span, SPANS), (chord, CHORDS))[axis]
        there = place + 2 * side
        pl.when(jnp.logical_and(there > 0, there <= count))(act)

    me_in = (chord * 2 + core, chip)

    def partner(phase, off):
        there = lax.rem(me_in[phase] + off, GROUP)
        if phase == 0:
            return (chip * 2 + lax.rem(there, 2), there // 2)
        return (there * 2 + core, chord)

    barrier = pltpu.get_barrier_semaphore()
    for side in (0, 1):
        pl.semaphore_signal(barrier, inc=1, device_id=neighbour(0, side), device_id_type=MESH)
    for phase in range(2):
        for off in range(1, GROUP):
            pl.semaphore_signal(
                barrier, inc=1, device_id=partner(phase, off), device_id_type=MESH
            )

    basis[...] = jnp.zeros_like(basis)
    adj[...] = jnp.zeros_like(adj)
    gacc[...] = jnp.zeros_like(gacc)
    for copy in small_copies[:2]:
        copy.wait()
    alive = lax.broadcasted_iota(jnp.int32, (8, ELEMS), 1) < live[0]
    alive6 = alive[:NVAR]
    lane6 = lax.broadcasted_iota(jnp.int32, (NVAR, ELEMS), 1)
    eye = lax.broadcasted_iota(jnp.int32, (GROUP, ELEMS), 0) == lax.broadcasted_iota(
        jnp.int32, (GROUP, ELEMS), 1
    )
    masks[0] = jnp.where(alive, 1.0, 0.0)
    vars6 = pl.ds(0, NVAR)
    for node in range(NODES):
        rows = pl.ds(node, NVAR, stride=NODES)
        basis[0, node, vars6, :] = jnp.where(alive6, rhs[rows, :], 0.0)
    for copy in small_copies[2:]:
        copy.wait()
    thetas = [shifts[order[k]] for k in range(STEPS)]

    def remote(step, axis, side):
        g, there = 2 * axis + side, 2 * axis + 1 - side
        return pltpu.make_async_remote_copy(
            src_ref=sbuf.at[step, g],
            dst_ref=rbuf.at[step, there],
            send_sem=send_sem.at[step, g],
            recv_sem=recv_sem.at[step, there],
            device_id=neighbour(axis, side),
            device_id_type=MESH,
        )

    def face_products(k, faces, first, unroll):
        def some(v, sums):
            sums = list(sums)
            for j in range(9):
                for n, (axis, side) in enumerate(faces):
                    g = 2 * axis + side
                    if first:
                        block = fstage[g, v * 9 + j].astype(F32)
                        face[g, v * 9 + j] = block
                    else:
                        block = face[g, v * 9 + j]
                    sums[n] = sums[n] + block * basis[k, node_of(axis, side, j), pl.ds(v, 1), :]
            return tuple(sums)

        def body(i, sums):
            for u in range(unroll):
                sums = some(i * unroll + u, sums)
            return sums

        zero = tuple(jnp.zeros((FACE, ELEMS), F32) for _ in faces)
        if unroll == NVAR:
            return body(0, zero)
        return lax.fori_loop(0, NVAR // unroll, body, zero)

    def oriented(g, product):
        prod[g, pl.ds(0, FACE), :] = product
        y = [[prod[g, pl.ds(3 * s + t, NVAR, stride=9), :] for t in range(3)] for s in range(3)]
        code = jnp.broadcast_to(codes[pl.ds(g, 1), :], (NVAR, ELEMS))
        swap, flip_s, flip_t = [(code & bit) != 0 for bit in (4, 1, 2)]
        y = [[y[s][t] if s == t else jnp.where(swap, y[t][s], y[s][t]) for t in range(3)] for s in range(3)]
        y = [[y[s][t] if s == 1 else jnp.where(flip_s, y[2 - s][t], y[s][t]) for t in range(3)] for s in range(3)]
        y = [[y[s][t] if t == 1 else jnp.where(flip_t, y[s][2 - t], y[s][t]) for t in range(3)] for s in range(3)]
        return [y[j // 3][j % 3] for j in range(9)]

    def send_face(step, k, axis, side, first):
        g = 2 * axis + side
        (product,) = face_products(k, ((axis, side),), first, 1 if first else NVAR)
        for j, value in enumerate(oriented(g, product)):
            sbuf[step, g, j] = value
        when_there(axis, side, lambda: remote(step, axis, side).start())

    def local_faces(k, first):
        products = face_products(k, ((2, 0), (2, 1)), first, 1 if first else 3)
        for j, value in enumerate(oriented(5, products[1])):
            local[0, j] = jnp.where(lane6 == 0, 0.0, pltpu.roll(value, 1, 1))
        for j, value in enumerate(oriented(4, products[0])):
            local[1, j] = jnp.where(lane6 == ELEMS - 1, 0.0, pltpu.roll(value, ELEMS - 1, 1))

    def diag_product(k, first):
        def body(v, total):
            if first:
                diag_copy(v).wait()
            for node in range(NODES):
                p = v * NODES + node
                if first:
                    block = dstage[p].astype(F32)
                    diag[p] = block
                else:
                    block = diag[p]
                total = total + block * basis[k, node, pl.ds(v, 1), :]
            return total

        result[...] = lax.fori_loop(0, NVAR, body, jnp.zeros((BLOCK, ELEMS), F32))

    def own_part(k, theta):
        for node in range(NODES):
            c = node % 3
            value = result[pl.ds(node, NVAR, stride=NODES), :]
            if c != 1:
                value = value + local[c // 2, node // 3]
            value = jnp.where(alive6, value, 0.0)
            basis[k + 1, node, vars6, :] = value - theta * basis[k, node, vars6, :]

    def arrive(step, to, axis, side):
        def act():
            remote(step, axis, 1 - side).wait_recv()
            mask = masks[1, vars6, :]
            for j in range(9):
                at = node_of(axis, side, j)
                got = rbuf[step, 2 * axis + side, j]
                basis[to, at, vars6, :] = basis[to, at, vars6, :] + mask * got

        when_there(axis, side, act)

    def sent(step):
        for one in (far, middle, outer, near):
            when_there(*one, remote(step, *one).wait_send)

    def phase_copy(cycle, phase, off, count=None):
        place = pl.ds(0, count) if count else me_in[phase]
        ref = slots.at[cycle, phase, place]
        return pltpu.make_async_remote_copy(
            src_ref=ref,
            dst_ref=ref,
            send_sem=gsend_sem.at[cycle, phase],
            recv_sem=grecv_sem.at[cycle, phase],
            device_id=partner(phase, off),
            device_id_type=MESH,
        )

    def send_phase(cycle, phase, row):
        slots[cycle, phase, me_in[phase]] = row
        for off in range(1, GROUP):
            phase_copy(cycle, phase, off).start()

    def take_phase(cycle, phase):
        copy = phase_copy(cycle, phase, 1, GROUP - 1)
        copy.wait_recv()
        copy.wait_send()
        return jnp.sum(slots[cycle, phase], axis=0)

    def start_gram(cycle):
        def body(i, sums):
            sums = list(sums)
            for u in range(3):
                v = [basis[k, i * 3 + u] for k in range(5)]
                for a in range(5):
                    for b in range(a, 5):
                        e = pair_index(a, b)
                        sums[e] = sums[e] + v[a] * v[b]
            return tuple(sums)

        sums = lax.fori_loop(
            0, NODES // 3, body, tuple(jnp.zeros((8, ELEMS), F32) for _ in range(ENTRIES))
        )
        for e in range(ENTRIES):
            gacc[pl.ds(8 * e, 8), :] = sums[e]
        part = gacc[pl.ds(0, GROUP, stride=8), :]
        for r in range(1, 8):
            part = part + gacc[pl.ds(r, GROUP, stride=8), :]
        column = jnp.sum(part, axis=1, keepdims=True)
        row = jnp.sum(jnp.where(eye, column, 0.0), axis=0, keepdims=True)
        send_phase(cycle, 0, row)

    def middle_gram(cycle):
        send_phase(cycle, 1, take_phase(cycle, 0))

    def end_gram(cycle):
        row = take_phase(cycle, 1)
        spread = jnp.sum(jnp.where(eye, row, 0.0), axis=1, keepdims=True)
        spread = jnp.broadcast_to(spread, (GROUP, ELEMS))
        gram = [
            [spread[pair_index(i, j):pair_index(i, j) + 1] for j in range(5)] for i in range(5)
        ]
        half = [[gram[i][k] * thetas[k] + gram[i][k + 1] for k in range(4)] for i in range(5)]
        normal = [[half[j][k] * thetas[j] + half[j + 1][k] for k in range(4)] for j in range(4)]
        target = [gram[j][0] * thetas[j] + gram[j + 1][0] for j in range(4)]
        low = [[None] * 4 for _ in range(4)]
        scaled = [[None] * 4 for _ in range(4)]
        inverse = [None] * 4
        for j in range(4):
            for i in range(j, 4):
                value = normal[i][j]
                for m in range(j):
                    value = value - low[j][m] * scaled[i][m]
                scaled[i][j] = value
            inverse[j] = 1.0 / scaled[j][j]
            for i in range(j + 1, 4):
                low[i][j] = scaled[i][j] * inverse[j]
        fore = []
        for i in range(4):
            value = target[i]
            for m in range(i):
                value = value - low[i][m] * fore[m]
            fore.append(value)
        weights = [None] * 4
        for i in reversed(range(4)):
            value = fore[i] * inverse[i]
            for m in range(i + 1, 4):
                value = value - low[m][i] * weights[m]
            weights[i] = value
        combined = [weights[0] * thetas[0]]
        for i in range(1, 4):
            combined.append(weights[i] * thetas[i] + weights[i - 1])
        combined.append(weights[3])
        lanes = lax.broadcasted_iota(jnp.int32, (1, ELEMS), 1)
        line = jnp.zeros((1, ELEMS), F32)
        for i in range(4):
            line = jnp.where(lanes == i, weights[i], line)
        coef_out[pl.ds(cycle, 1), :] = line[:, :STEPS]
        return weights, combined

    def next_cycle(cycle):
        weights, combined = end_gram(cycle)
        sets = [[1.0 - combined[0]] + [-value for value in combined[1:]]]
        for m in range(AHEAD):
            old = sets[-1]
            new = [None] * (len(old) + 1)
            for i, value in enumerate(old):
                here = value * (thetas[i % STEPS] - thetas[m])
                new[i] = here if new[i] is None else new[i] + here
                new[i + 1] = value
            sets.append(new)
        factor = jnp.broadcast_to(sets[AHEAD][-1], (8, ELEMS))
        masks[1] = masks[0] * factor
        weights8, combined8 = wide(weights), wide(combined)
        sets8 = [wide(one) for one in sets[1:]]

        def body(i, carry):
            for u in range(3):
                at = i * 3 + u
                v = [basis[k, at] for k in range(STEPS + AHEAD + 1)]
                total = adj[at]
                for k in range(STEPS):
                    total = total + weights8[k] * v[k]
                adj[at] = total
                fresh = v[0]
                for k in range(STEPS + 1):
                    fresh = fresh - combined8[k] * v[k]
                basis[0, at] = fresh
                for m in range(AHEAD):
                    total = sets8[m][0] * v[0]
                    for k in range(1, len(sets8[m])):
                        total = total + sets8[m][k] * v[k]
                    basis[m + 1, at] = total
            return carry

        lax.fori_loop(0, NODES // 3, body, 0)

    def last_cycle(cycle):
        weights, combined = end_gram(cycle)
        weights6, combined6 = wide(weights, NVAR), wide(combined, NVAR)
        for node in range(NODES):
            rows = pl.ds(node, NVAR, stride=NODES)
            v = [basis[k, node, vars6, :] for k in range(STEPS + 1)]
            total = adj[node, vars6, :]
            for k in range(STEPS):
                total = total + weights6[k] * v[k]
            adj_out[rows, :] = total
            fresh = v[0]
            for k in range(STEPS + 1):
                fresh = fresh - combined6[k] * v[k]
            res_out[rows, :] = fresh

    def product(step, k, theta, first):
        for one in (far, middle, outer, near):
            if first:
                face_copy(*one).wait()
            if first and one is far:
                pl.semaphore_wait(barrier, 2 * GROUP)
            send_face(step, k, *one, first)
        to = k + 1
        if not first:
            sent(step - 1)
            place = lax.rem(step, 4)
            cycle = step // 4 - 1

            @pl.when(jnp.logical_and(place == 0, step >= STEPS))
            def _():
                start_gram(cycle)

        else:
            face_copy(2, 0).wait()
            face_copy(2, 1).wait()
        local_faces(k, first)
        diag_product(k, first)
        own_part(k, theta)
        masks[1] = masks[0]
        if not first:

            @pl.when(jnp.logical_and(place == 1, step >= STEPS))
            def _():
                middle_gram(cycle)

            @pl.when(jnp.logical_and(place == 3, step >= STEPS))
            def _():
                next_cycle(cycle)

            to = jnp.where(k == STEPS + AHEAD - 1, AHEAD, to)
        for one in (near, outer, middle, far):
            arrive(step, to, *one)

    product(0, 0, thetas[0], True)

    def step_body(step, carry):
        k = jnp.where(step < STEPS, step, lax.rem(step, STEPS) + STEPS)
        product(step, k, shifts[order[lax.rem(k, STEPS)]], False)
        return carry

    lax.fori_loop(1, TOTAL, step_body, 0)
    start_gram(CYCLES - 1)
    sent(TOTAL - 1)
    middle_gram(CYCLES - 1)
    last_cycle(CYCLES - 1)


def wide(values, rows=8):
    return [jnp.broadcast_to(value, (rows, ELEMS)) for value in values]


def copy_kernel(a, b, c, x, y, z):
    x[...] = a[...]
    y[...] = b[...]
    z[...] = c[...]


def hand_out(arrays):
    vmem = pl.BlockSpec(memory_space=pltpu.VMEM)
    return pl.pallas_call(
        copy_kernel,
        out_shape=tuple(jax.ShapeDtypeStruct(one.shape, one.dtype) for one in arrays),
        in_specs=[vmem] * 3,
        out_specs=(vmem,) * 3,
    )(*arrays)


def on_device(right_side, diag_blocks, face_blocks, orient_codes, live_counts, shifts, shift_order):
    vmem = pl.BlockSpec(memory_space=pltpu.VMEM)
    anywhere = pl.BlockSpec(memory_space=pl.ANY)
    arrays = pl.pallas_call(
        kernel,
        out_shape=(
            jax.ShapeDtypeStruct((BLOCK, ELEMS), F32),
            jax.ShapeDtypeStruct((BLOCK, ELEMS), F32),
            jax.ShapeDtypeStruct((CYCLES, STEPS), F32),
        ),
        in_specs=[anywhere] * 7,
        out_specs=(vmem, vmem, vmem),
        scratch_shapes=[
            pltpu.VMEM((BLOCK, BLOCK, ELEMS), jnp.bfloat16),
            pltpu.VMEM((6, FACE, FACE, ELEMS), jnp.bfloat16),
            pltpu.VMEM((BLOCK, BLOCK, ELEMS), F32),
            pltpu.VMEM((6, FACE, FACE, ELEMS), F32),
            pltpu.VMEM((BLOCK, ELEMS), F32),
            pltpu.VMEM((6, ELEMS), jnp.int32),
            pltpu.SMEM((1,), jnp.int32),
            pltpu.SMEM((STEPS,), F32),
            pltpu.SMEM((STEPS,), jnp.int32),
            pltpu.VMEM((STEPS + AHEAD + 1, NODES, 8, ELEMS), F32),
            pltpu.VMEM((NODES, 8, ELEMS), F32),
            pltpu.VMEM((6, 56, ELEMS), F32),
            pltpu.VMEM((BLOCK, ELEMS), F32),
            pltpu.VMEM((2, 9, NVAR, ELEMS), F32),
            pltpu.VMEM((2, 8, ELEMS), F32),
            pltpu.VMEM((TOTAL, 4, 9, NVAR, ELEMS), F32),
            pltpu.VMEM((TOTAL, 4, 9, NVAR, ELEMS), F32),
            pltpu.VMEM((GROUP * 8, ELEMS), F32),
            pltpu.VMEM((CYCLES, 2, GROUP, 1, ELEMS), F32),
            pltpu.SemaphoreType.DMA((5,)),
            pltpu.SemaphoreType.DMA((BLOCK // CHUNK,)),
            pltpu.SemaphoreType.DMA((6,)),
            pltpu.SemaphoreType.DMA((TOTAL, 4)),
            pltpu.SemaphoreType.DMA((TOTAL, 4)),
            pltpu.SemaphoreType.DMA((CYCLES, 2)),
            pltpu.SemaphoreType.DMA((CYCLES, 2)),
        ],
        compiler_params=pltpu.CompilerParams(
            collective_id=0, has_side_effects=True, vmem_limit_bytes=56 * 2**20
        ),
    )(right_side, diag_blocks, face_blocks, orient_codes, live_counts, shifts, shift_order)
    return hand_out(arrays)


def solution(mesh):
    placed = (
        P(None, ("span", "chord")),
        P(None, None, ("span", "chord")),
        P(None, None, None, ("span", "chord")),
        P(None, ("span", "chord")),
        P(("span", "chord")),
        P(),
        P(),
    )
    return jax.shard_map(
        on_device,
        mesh=mesh,
        in_specs=placed,
        out_specs=(P(None, ("span", "chord")), P(None, ("span", "chord")), P()),
        check_vma=False,
    )
```

time: 85 us -> 68.8 us (0.81)
  Pallas kernels: 79.2 us -> 67.4 us
  local copies, waits for them, and re-layouts: 4.29 us -> 0 us
    pallas_call x1, Pallas kernels: 79.2 us -> 65.8 us  [on_device(): pl.pallas_call(kernel, out_shape=(jax.ShapeDtypeStruct((BLOCK, ELEMS), F3...]
    unnamed x3 -> x0, local copies, waits for them, and re-layouts: 4.29 us -> none
    pallas_call x0 -> x1, Pallas kernels: none -> 1.61 us  [hand_out(): pl.pallas_call(copy_kernel, out_shape=tuple((jax.ShapeDtypeStruct(one.sha...]
where the time goes in v1:
time: 68.8 us; the launch traced here: 68.7 us
  Pallas kernels  67.4 us (98%)
  between operations  1.29 us (2%)
    pallas_call x1, Pallas kernels, on_device(): pl.pallas_call(kernel, out_shape=(jax.ShapeDtypeStruct((BLOCK, ELEMS), F3...  65.8 us
    pallas_call x1, Pallas kernels, hand_out(): pl.pallas_call(copy_kernel, out_shape=tuple((jax.ShapeDtypeStruct(one.sha...  1.61 us

profile of v1, /device:TPU:1, one launch (start us, length us, event | category | flops | bytes accessed | tf_op | source)
XLA Modules:
  0.0 68.7 jit_solution(3770899097944674770)
XLA Ops:
  1.3 65.8 %shard_map.94 = (f32[162,128]{1,0:T(8,128)}, f32[162,128]{1,0:T(8,128)}, f32[3,4]{1,0:T(4,128)}) custom-call(f32[162,128]{1,0:T(8,128)} %rhs_hbm.1, bf16[162,162,128]{2,1,0:T(8,128)(2,1)} %diag_hbm.1, bf16[6,54,54,128]{3,2,1,0:T(8,128)(2,1)} %face_hbm.1, s32[6,128]{1,0:T(8,128)} %codes_hbm.1, s32[1]{0:T(128)S(6)} %copy.10.live_hbm, f32[4]{0:T(128)} %shifts_hbm.1, ...), custom_call_target="tpu_custom_call" | custom-call | tf_op jit(solution)/shard_map/pallas_call | solution.py:452
  67.1 1.6 %shard_map.95 = (f32[162,128]{1,0:T(8,128)}, f32[162,128]{1,0:T(8,128)}, f32[3,4]{1,0:T(4,128)}) custom-call(f32[162,128]{1,0:T(8,128)} %get-tuple-element.6.a, f32[162,128]{1,0:T(8,128)} %get-tuple-element.7.b, f32[3,4]{1,0:T(4,128)} %get-tuple-element.8.c), custom_call_target="tpu_custom_call" | custom-call | tf_op jit(solution)/shard_map/pallas_call | solution.py:441

commit v2 on v1

--- a/solution.py
+++ b/solution.py
@@ -18,6 +18,7 @@
 FACE = 54
 NVAR = 6
 NODES = 27
+WIDE = 8 * NODES
 ELEMS = 128
 SPANS = 32
 CHORDS = 8
@@ -41,8 +42,8 @@
 def kernel(
     rhs_hbm, diag_hbm, face_hbm, codes_hbm, live_hbm, shifts_hbm, order_hbm,
     adj_out, res_out, coef_out,
-    dstage, fstage, diag, face, rhs, codes, live, shifts, order, basis, adj, prod, result, local, masks, sbuf, rbuf,
-    gacc, slots,
+    dstage, fstage, face, rhs, codes, live, shifts, order, basis, adj, prod, result, local, masks, sbuf, rbuf,
+    gacc, slots, lines, done,
     small_sem, dsem, fsem, send_sem, recv_sem, gsend_sem, grecv_sem,
 ):
     span, chord = lax.axis_index("span"), lax.axis_index("chord")
@@ -54,9 +55,9 @@
         pltpu.make_async_copy(source, target, small_sem.at[i])
         for i, (source, target) in enumerate(
             (
-                (rhs_hbm, rhs),
+                (rhs_hbm, rhs.at[pl.ds(0, BLOCK)]),
                 (live_hbm, live),
-                (codes_hbm, codes),
+                (codes_hbm, codes.at[pl.ds(0, 6)]),
                 (shifts_hbm, shifts),
                 (order_hbm, order),
             )
@@ -69,18 +70,7 @@
         g = 2 * axis + side
         return pltpu.make_async_copy(face_hbm.at[g], fstage.at[g], fsem.at[g])
 
-    face_copy(*far).start()
-    for copy in small_copies[2:]:
-        copy.start()
-    for one in (middle, outer, near, (2, 0), (2, 1)):
-        face_copy(*one).start()
-
-    def diag_copy(i):
-        rows = pl.ds(i * CHUNK, CHUNK)
-        return pltpu.make_async_copy(diag_hbm.at[rows], dstage.at[rows], dsem.at[i])
-
-    for i in range(BLOCK // CHUNK):
-        diag_copy(i).start()
+    face_copy(*middle).start()
 
     def neighbour(axis, side):
         if axis == 0:
@@ -108,6 +98,18 @@
             pl.semaphore_signal(
                 barrier, inc=1, device_id=partner(phase, off), device_id_type=MESH
             )
+
+    for copy in small_copies[2:]:
+        copy.start()
+    for one in (far, outer, near, (2, 0), (2, 1)):
+        face_copy(*one).start()
+
+    def diag_copy(i):
+        rows = pl.ds(i * CHUNK, CHUNK)
+        return pltpu.make_async_copy(diag_hbm.at[rows], dstage.at[rows], dsem.at[i])
+
+    for i in range(BLOCK // CHUNK):
+        diag_copy(i).start()
 
     basis[...] = jnp.zeros_like(basis)
     adj[...] = jnp.zeros_like(adj)
@@ -140,17 +142,18 @@
             device_id_type=MESH,
         )
 
-    def face_products(k, faces, first, unroll):
+    def face_products(k, faces, first, unroll, slot=None):
         def some(v, sums):
             sums = list(sums)
             for j in range(9):
                 for n, (axis, side) in enumerate(faces):
                     g = 2 * axis + side
-                    if first:
+                    if slot is not None and not first:
+                        block = face[slot, v * 9 + j]
+                    else:
                         block = fstage[g, v * 9 + j].astype(F32)
-                        face[g, v * 9 + j] = block
-                    else:
-                        block = face[g, v * 9 + j]
+                        if slot is not None:
+                            face[slot, v * 9 + j] = block
                     sums[n] = sums[n] + block * basis[k, node_of(axis, side, j), pl.ds(v, 1), :]
             return tuple(sums)
 
@@ -174,15 +177,17 @@
         y = [[y[s][t] if t == 1 else jnp.where(flip_t, y[s][2 - t], y[s][t]) for t in range(3)] for s in range(3)]
         return [y[j // 3][j % 3] for j in range(9)]
 
-    def send_face(step, k, axis, side, first):
+    def send_face(step, k, axis, side, first, slot):
         g = 2 * axis + side
-        (product,) = face_products(k, ((axis, side),), first, 1 if first else NVAR)
+        (product,) = face_products(k, ((axis, side),), first, NVAR, slot)
         for j, value in enumerate(oriented(g, product)):
             sbuf[step, g, j] = value
+        if first and slot == 0:
+            pl.semaphore_wait(barrier, 2 * GROUP)
         when_there(axis, side, lambda: remote(step, axis, side).start())
 
     def local_faces(k, first):
-        products = face_products(k, ((2, 0), (2, 1)), first, 1 if first else 3)
+        products = face_products(k, ((2, 0), (2, 1)), first, 3)
         for j, value in enumerate(oriented(5, products[1])):
             local[0, j] = jnp.where(lane6 == 0, 0.0, pltpu.roll(value, 1, 1))
         for j, value in enumerate(oriented(4, products[0])):
@@ -194,15 +199,11 @@
                 diag_copy(v).wait()
             for node in range(NODES):
                 p = v * NODES + node
-                if first:
-                    block = dstage[p].astype(F32)
-                    diag[p] = block
-                else:
-                    block = diag[p]
+                block = dstage[p].astype(F32)
                 total = total + block * basis[k, node, pl.ds(v, 1), :]
             return total
 
-        result[...] = lax.fori_loop(0, NVAR, body, jnp.zeros((BLOCK, ELEMS), F32))
+        result[pl.ds(0, BLOCK), :] = lax.fori_loop(0, NVAR, body, jnp.zeros((BLOCK, ELEMS), F32))
 
     def own_part(k, theta):
         for node in range(NODES):
@@ -319,7 +320,7 @@
         line = jnp.zeros((1, ELEMS), F32)
         for i in range(4):
             line = jnp.where(lanes == i, weights[i], line)
-        coef_out[pl.ds(cycle, 1), :] = line[:, :STEPS]
+        lines[pl.ds(cycle, 1), :] = line
         return weights, combined
 
     def next_cycle(cycle):
@@ -368,19 +369,21 @@
             total = adj[node, vars6, :]
             for k in range(STEPS):
                 total = total + weights6[k] * v[k]
-            adj_out[rows, :] = total
+            done[0, rows, :] = total
             fresh = v[0]
             for k in range(STEPS + 1):
                 fresh = fresh - combined6[k] * v[k]
-            res_out[rows, :] = fresh
+            done[1, rows, :] = fresh
+
+        adj_out[...] = done[0, pl.ds(0, BLOCK), :]
+        res_out[...] = done[1, pl.ds(0, BLOCK), :]
+        coef_out[...] = lines[pl.ds(0, CYCLES), :][:, :STEPS]
 
     def product(step, k, theta, first):
-        for one in (far, middle, outer, near):
+        for slot, one in ((0, middle), (1, far), (None, outer), (None, near)):
             if first:
                 face_copy(*one).wait()
-            if first and one is far:
-                pl.semaphore_wait(barrier, 2 * GROUP)
-            send_face(step, k, *one, first)
+            send_face(step, k, *one, first, slot)
         to = k + 1
         if not first:
             sent(step - 1)
@@ -409,7 +412,7 @@
                 next_cycle(cycle)
 
             to = jnp.where(k == STEPS + AHEAD - 1, AHEAD, to)
-        for one in (near, outer, middle, far):
+        for one in (near, outer, far, middle):
             arrive(step, to, *one)
 
     product(0, 0, thetas[0], True)
@@ -448,7 +451,7 @@
 
 def on_device(right_side, diag_blocks, face_blocks, orient_codes, live_counts, shifts, shift_order):
     vmem = pl.BlockSpec(memory_space=pltpu.VMEM)
-    anywhere = pl.BlockSpec(memory_space=pl.ANY)
+    hbm = pl.BlockSpec(memory_space=pltpu.HBM)
     arrays = pl.pallas_call(
         kernel,
         out_shape=(
@@ -456,28 +459,29 @@
             jax.ShapeDtypeStruct((BLOCK, ELEMS), F32),
             jax.ShapeDtypeStruct((CYCLES, STEPS), F32),
         ),
-        in_specs=[anywhere] * 7,
+        in_specs=[hbm] * 7,
         out_specs=(vmem, vmem, vmem),
         scratch_shapes=[
             pltpu.VMEM((BLOCK, BLOCK, ELEMS), jnp.bfloat16),
             pltpu.VMEM((6, FACE, FACE, ELEMS), jnp.bfloat16),
-            pltpu.VMEM((BLOCK, BLOCK, ELEMS), F32),
-            pltpu.VMEM((6, FACE, FACE, ELEMS), F32),
-            pltpu.VMEM((BLOCK, ELEMS), F32),
-            pltpu.VMEM((6, ELEMS), jnp.int32),
+            pltpu.VMEM((2, FACE, FACE, ELEMS), F32),
+            pltpu.VMEM((WIDE, ELEMS), F32),
+            pltpu.VMEM((16, ELEMS), jnp.int32),
             pltpu.SMEM((1,), jnp.int32),
             pltpu.SMEM((STEPS,), F32),
             pltpu.SMEM((STEPS,), jnp.int32),
             pltpu.VMEM((STEPS + AHEAD + 1, NODES, 8, ELEMS), F32),
             pltpu.VMEM((NODES, 8, ELEMS), F32),
-            pltpu.VMEM((6, 56, ELEMS), F32),
-            pltpu.VMEM((BLOCK, ELEMS), F32),
+            pltpu.VMEM((6, 72, ELEMS), F32),
+            pltpu.VMEM((WIDE, ELEMS), F32),
             pltpu.VMEM((2, 9, NVAR, ELEMS), F32),
             pltpu.VMEM((2, 8, ELEMS), F32),
             pltpu.VMEM((TOTAL, 4, 9, NVAR, ELEMS), F32),
             pltpu.VMEM((TOTAL, 4, 9, NVAR, ELEMS), F32),
             pltpu.VMEM((GROUP * 8, ELEMS), F32),
-            pltpu.VMEM((CYCLES, 2, GROUP, 1, ELEMS), F32),
+            pltpu.VMEM((CYCLES + 1, 2, GROUP, 1, ELEMS), F32),
+            pltpu.VMEM((16, ELEMS), F32),
+            pltpu.VMEM((2, WIDE, ELEMS), F32),
             pltpu.SemaphoreType.DMA((5,)),
             pltpu.SemaphoreType.DMA((BLOCK // CHUNK,)),
             pltpu.SemaphoreType.DMA((6,)),

time: 68.8 us -> 68.5 us (level)
  no operation moved by 1% of the time
where the time goes in v2:
time: 68.5 us; the launch traced here: 68.4 us
  Pallas kernels  67.1 us (98%)
  between operations  1.29 us (2%)
    pallas_call x1, Pallas kernels, on_device(): pl.pallas_call(kernel, out_shape=(jax.ShapeDtypeStruct((BLOCK, ELEMS), F3...  65.5 us
    pallas_call x1, Pallas kernels, hand_out(): pl.pallas_call(copy_kernel, out_shape=tuple((jax.ShapeDtypeStruct(one.sha...  1.61 us

profile of v2, /device:TPU:1, one launch (start us, length us, event | category | flops | bytes accessed | tf_op | source)
XLA Modules:
  0.0 68.4 jit_solution(15204158904069851962)
XLA Ops:
  1.3 65.5 %shard_map.94 = (f32[162,128]{1,0:T(8,128)}, f32[162,128]{1,0:T(8,128)}, f32[3,4]{1,0:T(4,128)}) custom-call(f32[162,128]{1,0:T(8,128)} %rhs_hbm.1, bf16[162,162,128]{2,1,0:T(8,128)(2,1)} %diag_hbm.1, bf16[6,54,54,128]{3,2,1,0:T(8,128)(2,1)} %face_hbm.1, s32[6,128]{1,0:T(8,128)} %codes_hbm.1, s32[1]{0:T(128)S(6)} %copy.10.live_hbm, f32[4]{0:T(128)} %shifts_hbm.1, ...), custom_call_target="tpu_custom_call" | custom-call | tf_op jit(solution)/shard_map/pallas_call | solution.py:455
  66.8 1.6 %shard_map.95 = (f32[162,128]{1,0:T(8,128)}, f32[162,128]{1,0:T(8,128)}, f32[3,4]{1,0:T(4,128)}) custom-call(f32[162,128]{1,0:T(8,128)} %get-tuple-element.6.a, f32[162,128]{1,0:T(8,128)} %get-tuple-element.7.b, f32[3,4]{1,0:T(4,128)} %get-tuple-element.8.c), custom_call_target="tpu_custom_call" | custom-call | tf_op jit(solution)/shard_map/pallas_call | solution.py:444

commit v3 on v2

--- a/solution.py
+++ b/solution.py
@@ -255,8 +255,8 @@
     def start_gram(cycle):
         def body(i, sums):
             sums = list(sums)
-            for u in range(3):
-                v = [basis[k, i * 3 + u] for k in range(5)]
+            for u in range(9):
+                v = [basis[k, i * 9 + u] for k in range(5)]
                 for a in range(5):
                     for b in range(a, 5):
                         e = pair_index(a, b)
@@ -264,7 +264,7 @@
             return tuple(sums)
 
         sums = lax.fori_loop(
-            0, NODES // 3, body, tuple(jnp.zeros((8, ELEMS), F32) for _ in range(ENTRIES))
+            0, NODES // 9, body, tuple(jnp.zeros((8, ELEMS), F32) for _ in range(ENTRIES))
         )
         for e in range(ENTRIES):
             gacc[pl.ds(8 * e, 8), :] = sums[e]

time: 68.5 us -> 68.5 us (level)
  no operation moved by 1% of the time
where the time goes in v3:
time: 68.5 us; the launch traced here: 68.3 us
  Pallas kernels  67 us (98%)
  between operations  1.29 us (2%)
    pallas_call x1, Pallas kernels, on_device(): pl.pallas_call(kernel, out_shape=(jax.ShapeDtypeStruct((BLOCK, ELEMS), F3...  65.4 us
    pallas_call x1, Pallas kernels, hand_out(): pl.pallas_call(copy_kernel, out_shape=tuple((jax.ShapeDtypeStruct(one.sha...  1.61 us

profile of v3, /device:TPU:1, one launch (start us, length us, event | category | flops | bytes accessed | tf_op | source)
XLA Modules:
  0.0 68.3 jit_solution(10401176639464330133)
XLA Ops:
  1.3 65.4 %shard_map.94 = (f32[162,128]{1,0:T(8,128)}, f32[162,128]{1,0:T(8,128)}, f32[3,4]{1,0:T(4,128)}) custom-call(f32[162,128]{1,0:T(8,128)} %rhs_hbm.1, bf16[162,162,128]{2,1,0:T(8,128)(2,1)} %diag_hbm.1, bf16[6,54,54,128]{3,2,1,0:T(8,128)(2,1)} %face_hbm.1, s32[6,128]{1,0:T(8,128)} %codes_hbm.1, s32[1]{0:T(128)S(6)} %copy.10.live_hbm, f32[4]{0:T(128)} %shifts_hbm.1, ...), custom_call_target="tpu_custom_call" | custom-call | tf_op jit(solution)/shard_map/pallas_call | solution.py:455
  66.7 1.6 %shard_map.95 = (f32[162,128]{1,0:T(8,128)}, f32[162,128]{1,0:T(8,128)}, f32[3,4]{1,0:T(4,128)}) custom-call(f32[162,128]{1,0:T(8,128)} %get-tuple-element.6.a, f32[162,128]{1,0:T(8,128)} %get-tuple-element.7.b, f32[3,4]{1,0:T(4,128)} %get-tuple-element.8.c), custom_call_target="tpu_custom_call" | custom-call | tf_op jit(solution)/shard_map/pallas_call | solution.py:444
